TPU v7x, 768 devices: a whole 4x8x12 slice. The times are simulated.
768 devices in a mesh: grid: 48 (over z, y_lo, core), tp: 16 (over x, y_hi).
Axes of the slice: x: 4, y: 8 (y_hi: 4, y_lo: 2; y = y_hi * 2 + y_lo), z: 12, core: 2. Of those that a mesh axis runs over, the one named last changes fastest.
Arguments:
- latents: bfloat16 [18432, 3072], P('grid'), may hold values from -6 to 6
- input_weight: bfloat16 [3072, 6144], P('grid', 'tp'), as said below
- norm_gains: float32 [2, 128], replicated, as said below
- text_pairs: bfloat16 [256, 4096], P(None, 'tp'), may hold values from -6 to 6
- text_count: int32 [1], replicated, may hold values from 64 to 256
- output_weight: bfloat16 [2048, 3072], P('tp', 'grid'), may hold values from -0.125 to 0.125
Outputs:
- block_output: bfloat16 [18432, 3072], P('grid', 'tp')
Inputs may be any that keep to these rules, and one draw needn't show every extreme that they name: `text_count`: number of valid text tokens; the remaining text slots are padding. `input_weight`: a projection scaled by its fan-in. `norm_gains`: positive gains.
All inputs are finite; a program needn't handle non-finite values.
Results may differ from a plain program's by a relative error of at most 0.015.
Values may be sent and summed in bfloat16 or wider, within the bound.
A program may use at most 32 MiB of HBM per device.

v0:
```python
import jax
import jax.numpy as jnp
import numpy as np
from jax import lax
from jax.sharding import PartitionSpec as P

GRID_H = 4
TILE = 384


epsilon = 1e-06


def shifted(x, axis, by):
    length = lax.axis_size(axis)
    pairs = [(i, i + by) for i in range(length) if 0 <= i + by < length]
    return lax.ppermute(x, axis, pairs)


def root_norm(values, gain):
    return values * lax.rsqrt(jnp.mean(values * values, axis=-1, keepdims=True) + epsilon) * gain


def local(latents, input_weight, norm_gains, text_pairs, text_count, output_weight):
    row_count = latents.shape[0]
    in_width = input_weight.shape[1]
    head_size = norm_gains.shape[1]
    head_count = in_width // (3 * head_size)
    tile_rows = TILE
    tiles_wide = row_count // tile_rows
    projected = jnp.dot(
        latents,
        lax.all_gather(input_weight, "grid", axis=0, tiled=True),
        preferred_element_type=jnp.float32,
    )
    projected = projected.reshape(row_count, head_count, 3, head_size)
    queries = root_norm(projected[:, :, 0], norm_gains[0]).astype(jnp.bfloat16)
    key_rows = root_norm(projected[:, :, 1], norm_gains[1]).astype(jnp.bfloat16)
    values = projected[:, :, 2].astype(jnp.bfloat16)
    stacked = jnp.concatenate(
        [
            key_rows.reshape(row_count, head_count * head_size),
            values.reshape(row_count, head_count * head_size),
        ],
        axis=1,
    )
    offsets = [(step_time, step_height) for step_time in (-1, 0, 1) for step_height in (-1, 0, 1)]
    neighbours = []
    for step_time, step_height in offsets:
        if step_time == 0 and step_height == 0:
            neighbours.append(stacked)
        else:
            neighbours.append(shifted(stacked, "grid", -(step_time * GRID_H + step_height)))
    planes = jnp.stack(neighbours)
    grid_time = lax.axis_size("grid") // GRID_H
    place = lax.axis_index("grid")
    time_here = place // GRID_H
    height_here = place % GRID_H
    plane_ok = jnp.stack(
        [
            (time_here + step_time >= 0)
            & (time_here + step_time < grid_time)
            & ((height_here + step_height >= 0) & (height_here + step_height < GRID_H))
            for step_time, step_height in offsets
        ]
    )
    width_keep = min(3, tiles_wide)
    starts = np.clip(np.arange(tiles_wide) - 1, 0, tiles_wide - width_keep)
    width_index = starts[:, None] + np.arange(width_keep)[None, :]
    width_ok = np.abs(width_index - np.arange(tiles_wide)[:, None]) <= 1
    window_rows = 9 * width_keep * tile_rows
    planes = planes.reshape(9, tiles_wide, tile_rows, 2 * head_count * head_size)
    window = (
        planes[:, width_index]
        .transpose(1, 0, 2, 3, 4)
        .reshape(tiles_wide, window_rows, 2, head_count, head_size)
    )
    key_window = window[:, :, 0]
    value_window = window[:, :, 1]
    live = plane_ok[None, :, None, None] & jnp.asarray(width_ok)[:, None, :, None]
    live = jnp.broadcast_to(live, (tiles_wide, 9, width_keep, tile_rows)).reshape(
        tiles_wide, window_rows
    )
    text = text_pairs.reshape(text_pairs.shape[0], head_count, 2, head_size)
    text_keys = root_norm(text[:, :, 0].astype(jnp.float32), norm_gains[1]).astype(jnp.bfloat16)
    text_values = text[:, :, 1]
    live_text = jnp.arange(text_pairs.shape[0]) < text_count[0]
    score_scale = head_size ** (-0.5)
    query_tiles = queries.reshape(tiles_wide, tile_rows, head_count, head_size)
    video_scores = (
        jnp.einsum("wqhd,wkhd->whqk", query_tiles, key_window, preferred_element_type=jnp.float32)
        * score_scale
    )
    text_scores = (
        jnp.einsum("wqhd,khd->whqk", query_tiles, text_keys, preferred_element_type=jnp.float32)
        * score_scale
    )
    video_scores = jnp.where(live[:, None, None, :], video_scores, -jnp.inf)
    text_scores = jnp.where(live_text[None, None, None, :], text_scores, -jnp.inf)
    row_max = jnp.maximum(video_scores.max(-1), text_scores.max(-1))[..., None]
    video_exp = jnp.exp(video_scores - row_max)
    text_exp = jnp.exp(text_scores - row_max)
    denominator = video_exp.sum(-1, keepdims=True) + text_exp.sum(-1, keepdims=True)
    video_weights = (video_exp / denominator).astype(jnp.bfloat16)
    text_weights = (text_exp / denominator).astype(jnp.bfloat16)
    mixed = jnp.einsum(
        "whqk,wkhd->wqhd", video_weights, value_window, preferred_element_type=jnp.float32
    )
    mixed = mixed + jnp.einsum(
        "whqk,khd->wqhd", text_weights, text_values, preferred_element_type=jnp.float32
    )
    attention = mixed.astype(jnp.bfloat16).reshape(row_count, head_count * head_size)
    term = jnp.dot(
        attention,
        lax.all_gather(output_weight, "grid", axis=1, tiled=True),
        preferred_element_type=jnp.float32,
    )
    return lax.psum_scatter(term.astype(jnp.bfloat16), "tp", scatter_dimension=1, tiled=True)


def solution(mesh):
    placed = (P("grid", None), P("grid", "tp"), P(), P(None, "tp"), P(), P("tp", "grid"))
    return jax.shard_map(
        local, mesh=mesh, in_specs=placed, out_specs=P("grid", "tp"), check_vma=False
    )
```

profile of v0, /device:TPU:6, one launch (start us, length us, event | category | flops | bytes accessed | tf_op | source)
XLA Modules:
  0.0 280.8 jit_solution(13550001927839331310)
XLA Ops:
  6.5 0.7 all-gather.2.cloned.1.call-update
  7.3 0.0 reduce-scatter.2.cloned.1.call-start
  7.4 0.1 stack.79
  7.5 0.1 broadcast_in_dim.44
  7.6 1.0 copy.16
  8.6 0.0 copy-start.4
  9.3 0.5 iota_compare_fusion
  9.8 0.8 slice_bitcast_fusion.2
  10.6 0.6 add_rsqrt_fusion.2
  11.2 64.8 %all_gather.7 = bf16[128,3072]{0,1:T(8,128)(2,1)} all-gather(bf16[128,64]{0,1:T(8,128)(2,1)} %param.14), channel_id=1, replica_groups=mesh['grid'=48,'tp'=16] {'grid'}, dimensions={1}, use_global_device_ids=true | all-gather | bytes 802816 | tf_op jit(solution)/shard_map/all_gather | solution.py:115
  75.9 38.6 %all-gather.2.cloned.1.call-done = bf16[3072,384]{1,0:T(8,128)(2,1)} async-done(((bf16[64,384]{1,0:T(8,128)(2,1)}), bf16[3072,384]{1,0:T(8,128)(2,1)}) %all-gather.2.cloned.1.call-update) | async-done | bytes 2359312 | tf_op jit(solution)/shard_map/all_gather | solution.py:33
  114.5 3.1 %fusion.34 = f32[384,384]{0,1:T(8,128)S(1)} fusion(bf16[384,3072]{1,0:T(8,128)(2,1)S(1)} %copy-done, bf16[3072,384]{1,0:T(8,128)(2,1)} %all-gather.2.cloned.1.call-done), kind=kOutput, calls=%fused_computation.61 | convolution fusion | flops 905969664 | bytes 5308416 | tf_op jit(solution)/shard_map/dot_general | solution.py:31
  117.7 0.1 copy.23
  117.8 0.1 multiply_reduce_fusion.1
  118.0 0.1 copy.24
  118.1 0.1 fusion.18
  118.3 2.3 collective-permute-start
  120.6 2.8 collective-permute-start.1
  123.4 3.7 %collective-permute-start.2 = (bf16[384,256]{1,0:T(8,128)(2,1)S(1)}, bf16[384,256]{1,0:T(8,128)(2,1)S(1)}, u32[]{:S(2)}, u32[]{:S(2)}) collective-permute-start(bf16[384,256]{1,0:T(8,128)(2,1)S(1)} %pad_maximum_fusion), channel_id=1, source_target_pairs={{0,48},{16,64},{32,80},{48,96},{64,112},{80,128},{96,144},{112,160... | collective-permute-start | bytes 589832 | tf_op jit(solution)/shard_map/ppermute | solution.py:17
  127.0 1.5 collective-permute-start.3
  128.6 1.3 collective-permute-start.4
  129.9 1.9 fusion.33
  131.8 1.3 collective-permute-start.5
  133.1 0.7 bitcast_dynamic-update-slice_fusion.8
  133.8 1.3 collective-permute-start.6
  135.1 0.7 bitcast_dynamic-update-slice_fusion.7
  135.7 0.0 collective-permute-done.2
  135.8 1.3 collective-permute-start.7
  137.0 0.7 bitcast_dynamic-update-slice_fusion.6
  137.7 0.7 bitcast_dynamic-update-slice_fusion.5
  138.4 0.7 bitcast_dynamic-update-slice_fusion.4
  139.1 0.7 bitcast_dynamic-update-slice_fusion.3
  139.8 1.4 collective-permute-done.5
  141.2 0.7 bitcast_dynamic-update-slice_fusion.2
  141.9 6.9 %collective-permute-done.6 = bf16[384,256]{1,0:T(8,128)(2,1)S(1)} collective-permute-done((bf16[384,256]{1,0:T(8,128)(2,1)S(1)}, bf16[384,256]{1,0:T(8,128)(2,1)S(1)}, u32[]{:S(2)}, u32[]{:S(2)}) %collective-permute-start.6) | collective-permute-done | bytes 196640 | tf_op jit(solution)/shard_map/ppermute | solution.py:17
  148.8 0.7 bitcast_dynamic-update-slice_fusion.1
  149.5 2.5 collective-permute-done.7
  151.9 0.7 bitcast_dynamic-update-slice_fusion
  152.6 4.5 %reshape_transpose.3 = bf16[1,3456,2,1,128]{4,2,1,3,0:T(2,128)(2,1)} reshape(bf16[9,384,256]{2,1,0:T(8,128)(2,1)} %bitcast_dynamic-update-slice_fusion) | data formatting | bytes 3538944 | tf_op jit(solution)/shard_map/reshape;transpose | solution.py:76
  157.1 5.8 %fusion.30 = (bf16[1,3456,1,1,128]{4,2,1,3,0:T(2,128)(2,1)}, bf16[1,3456,1,1,128]{4,2,1,3,0:T(2,128)(2,1)S(1)}) fusion(bf16[1,3456,2,1,128]{4,2,1,3,0:T(2,128)(2,1)} %reshape_transpose.3), kind=kLoop, calls=%fused_computation.57 | loop fusion | bytes 3538944 | tf_op jit(solution)/shard_map/slice | solution.py:79
  163.0 1.1 fusion.32
  164.1 0.1 fusion.15
  164.2 0.9 fusion.1
  165.0 1.3 copy-done.1
  166.4 0.2 convolution_bitcast_fusion
  166.6 6.7 %convolution_convert_fusion = bf16[384,3072]{0,1:T(8,128)(2,1)} fusion(bf16[128,3072]{0,1:T(8,128)(2,1)S(1)} %copy-done.2, f32[1,384,1,128]{1,3,2,0:T(8,128)S(1)} %convolution_bitcast_fusion, f32[384,3456]{1,0:T(8,128)} %copy-done.1, f32[384]{0:T(512)S(1)} %add.90, f32[384]{0:T(512)S(1)} %max.9, bf16[1,3456,1,1,128]{4,2,1,3,0:T(2,128)(2,1)} %get-tuple-element.5), kind=kOutput, calls=%fused_computation.5 | convolution fusion | flops 646987776 | bytes 9538560 | tf_op jit(solution)/shard_map/dot_general | solution.py:113
  173.3 0.0 reduce-scatter.2.cloned.1.call-update
  173.3 100.6 %reduce-scatter.2.cloned.1.call-done = bf16[384,192]{0,1:T(8,128)(2,1)} async-done(((bf16[384,3072]{0,1:T(8,128)(2,1)}), bf16[384,192]{0,1:T(8,128)(2,1)}) %reduce-scatter.2.cloned.1.call-update) | async-done | bytes 147472 | tf_op jit(solution)/shard_map/reduce_scatter | solution.py:118
  (24 shorter events, 0.2 us)
Async XLA Ops:
  6.5 108.0 %copy-start = (bf16[384,3072]{1,0:T(8,128)(2,1)S(1)}, bf16[384,3072]{1,0:T(8,128)(2,1)}, u32[]{:S(2)}) copy-start(bf16[384,3072]{1,0:T(8,128)(2,1)} %param.9) | copy-start | bytes 7077892
  6.5 108.0 %all-gather.2.cloned.1.call-start = ((), (), s32[]{:S(2)}) async-start(), calls=%async_computation.1 | async-start | bytes 2408448 | tf_op jit(solution)/shard_map/all_gather | solution.py:33
  7.3 266.7 %reduce-scatter.2.cloned.1.call-start = ((), (), s32[]{:S(2)}) async-start(), calls=%async_computation.2 | async-start | bytes 2506752 | tf_op jit(solution)/shard_map/reduce_scatter | solution.py:118
  8.6 67.3 %copy-start.4 = (bf16[256,256]{0,1:T(8,128)(2,1)}, bf16[256,256]{0,1:T(8,128)(2,1)S(1)}, u32[]{:S(2)}) copy-start(bf16[256,256]{0,1:T(8,128)(2,1)S(1)} %copy.16) | copy-start | bytes 393220
  118.3 13.5 %collective-permute-start = (bf16[384,256]{1,0:T(8,128)(2,1)S(1)}, bf16[384,256]{1,0:T(8,128)(2,1)S(1)}, u32[]{:S(2)}, u32[]{:S(2)}) collective-permute-start(bf16[384,256]{1,0:T(8,128)(2,1)S(1)} %pad_maximum_fusion), channel_id=1, source_target_pairs={{0,80},{16,96},{32,112},{48,128},{64,144},{80,160},{96,176},{112,1... | collective-permute-start | bytes 589832 | tf_op jit(solution)/shard_map/ppermute | solution.py:17
  120.6 13.2 %collective-permute-start.1 = (bf16[384,256]{1,0:T(8,128)(2,1)S(1)}, bf16[384,256]{1,0:T(8,128)(2,1)S(1)}, u32[]{:S(2)}, u32[]{:S(2)}) collective-permute-start(bf16[384,256]{1,0:T(8,128)(2,1)S(1)} %pad_maximum_fusion), channel_id=1, source_target_pairs={{0,64},{16,80},{32,96},{48,112},{64,128},{80,144},{96,160},{112,17... | collective-permute-start | bytes 589832 | tf_op jit(solution)/shard_map/ppermute | solution.py:17
  123.4 12.4 %collective-permute-start.2 = (bf16[384,256]{1,0:T(8,128)(2,1)S(1)}, bf16[384,256]{1,0:T(8,128)(2,1)S(1)}, u32[]{:S(2)}, u32[]{:S(2)}) collective-permute-start(bf16[384,256]{1,0:T(8,128)(2,1)S(1)} %pad_maximum_fusion), channel_id=1, source_target_pairs={{0,48},{16,64},{32,80},{48,96},{64,112},{80,128},{96,144},{112,160... | collective-permute-start | bytes 589832 | tf_op jit(solution)/shard_map/ppermute | solution.py:17
  127.0 10.7 %collective-permute-start.3 = (bf16[384,256]{1,0:T(8,128)(2,1)S(1)}, bf16[384,256]{1,0:T(8,128)(2,1)S(1)}, u32[]{:S(2)}, u32[]{:S(2)}) collective-permute-start(bf16[384,256]{1,0:T(8,128)(2,1)S(1)} %pad_maximum_fusion), channel_id=1, source_target_pairs={{0,16},{16,32},{32,48},{48,64},{64,80},{80,96},{96,112},{112,128},... | collective-permute-start | bytes 589832 | tf_op jit(solution)/shard_map/ppermute | solution.py:17
  128.6 10.6 %collective-permute-start.4 = (bf16[384,256]{1,0:T(8,128)(2,1)S(1)}, bf16[384,256]{1,0:T(8,128)(2,1)S(1)}, u32[]{:S(2)}, u32[]{:S(2)}) collective-permute-start(bf16[384,256]{1,0:T(8,128)(2,1)S(1)} %pad_maximum_fusion), channel_id=1, source_target_pairs={{16,0},{32,16},{48,32},{64,48},{80,64},{96,80},{112,96},{128,112},... | collective-permute-start | bytes 589832 | tf_op jit(solution)/shard_map/ppermute | solution.py:17
  131.8 9.4 %collective-permute-start.5 = (bf16[384,256]{1,0:T(8,128)(2,1)S(1)}, bf16[384,256]{1,0:T(8,128)(2,1)S(1)}, u32[]{:S(2)}, u32[]{:S(2)}) collective-permute-start(bf16[384,256]{1,0:T(8,128)(2,1)S(1)} %pad_maximum_fusion), channel_id=1, source_target_pairs={{48,0},{64,16},{80,32},{96,48},{112,64},{128,80},{144,96},{160,112... | collective-permute-start | bytes 589832 | tf_op jit(solution)/shard_map/ppermute | solution.py:17
  133.8 15.0 %collective-permute-start.6 = (bf16[384,256]{1,0:T(8,128)(2,1)S(1)}, bf16[384,256]{1,0:T(8,128)(2,1)S(1)}, u32[]{:S(2)}, u32[]{:S(2)}) collective-permute-start(bf16[384,256]{1,0:T(8,128)(2,1)S(1)} %pad_maximum_fusion), channel_id=1, source_target_pairs={{64,0},{80,16},{96,32},{112,48},{128,64},{144,80},{160,96},{176,11... | collective-permute-start | bytes 589832 | tf_op jit(solution)/shard_map/ppermute | solution.py:17
  135.8 16.2 %collective-permute-start.7 = (bf16[384,256]{1,0:T(8,128)(2,1)S(1)}, bf16[384,256]{1,0:T(8,128)(2,1)S(1)}, u32[]{:S(2)}, u32[]{:S(2)}) collective-permute-start(bf16[384,256]{1,0:T(8,128)(2,1)S(1)} %pad_maximum_fusion), channel_id=1, source_target_pairs={{80,0},{96,16},{112,32},{128,48},{144,64},{160,80},{176,96},{192,1... | collective-permute-start | bytes 589832 | tf_op jit(solution)/shard_map/ppermute | solution.py:17
  162.9 1.1 copy-start.3
  164.0 2.3 copy-start.1
  164.2 2.2 copy-start.5
  164.2 2.4 copy-start.2
Sparse Core Ops, SparseCore 0:
  9.8 104.6 all-gather.1
  173.5 100.4 reduce-scatter.1
where the time goes:
time: 282 us; the launch traced here: 281 us
  waiting for transfers between devices  151 us (54%)
  blocking collectives  64.8 us (23%)
  local copies, waits for them, and re-layouts  19.4 us (7%)
  starting transfers between devices  15.4 us (5%)
  between operations  14.3 us (5%)
  matrix products  13 us (5%)
  other arithmetic  3.13 us (1%)
    reduce_scatter x1, waiting for transfers between devices, local(): lax.psum_scatter(term.astype(jnp.bfloat16), 'tp', scatter_dimension=1, ti...  101 us
    all_gather x1, blocking collectives, local(): lax.all_gather(output_weight, 'grid', axis=1, tiled=True)  64.8 us
    all_gather x1, waiting for transfers between devices, local(): lax.all_gather(input_weight, 'grid', axis=0, tiled=True)  38.6 us
    ppermute x8, starting transfers between devices, shifted(): return lax.ppermute(x, axis, pairs)  15.4 us
    ppermute x8, waiting for transfers between devices, shifted(): return lax.ppermute(x, axis, pairs)  10.7 us
    unnamed x22, local copies, waits for them, and re-layouts  7.46 us
    dot_general x1, matrix products, local(): jnp.dot(attention, lax.all_gather(output_weight, 'grid', axis=1, tiled=Tr...  6.72 us
    slice x1, local copies, waits for them, and re-layouts, local(): value_window = window[:, :, 1]  5.84 us
  transfers between devices with their start and end apart: 10, of which 5 were waited for; matrix products, arithmetic and copies ran while one was open for 4% of the time, Pallas kernels for 0%

commit v1 on v0

v1 whole, which is shorter than its diff:
```python
import functools

import jax
import jax.numpy as jnp
from jax import lax
from jax.experimental import pallas as pl
from jax.experimental.pallas import tpu as pltpu
from jax.sharding import PartitionSpec as P

NZ = 12
NX = 4
NYH = 4
TILE = 384
HD = 128
RANK = 64
BLOCKS = 3
ROWS = TILE // BLOCKS
OUT = 192
EPS = 1e-6
MESH = pl.DeviceIdType.MESH
NT = (((1,), (1,)), ((), ()))
F32 = jnp.float32
BF16 = jnp.bfloat16


def rms(values, gain):
    return values * lax.rsqrt(jnp.mean(values * values, axis=-1, keepdims=True) + EPS) * gain


def chunks_of(step):
    if step == 0:
        return [0]
    if step == NZ // 2:
        return [NZ - 1]
    return [2 * step - 1, 2 * step]


def kernel(
    lat_hbm, win_hbm, gains, text, count, wout_hbm, out,
    lat, w, w2, piece, acc, q, kv, m, l, o, att, part, send, got,
    local_sem, perm_sem,
    wz_s, wz_r, wy_s, wy_r, wc_s, wc_r,
    vz_s, vz_r, vy_s, vy_r, vc_s, vc_r,
    kz_s, kz_r, ky_s, ky_r, kc_s, kc_r,
    at_s, at_r, rs_s, rs_r,
):
    g = lax.axis_index("grid")
    t = lax.axis_index("tp")
    z, yl, c = g // 4, (g // 2) % 2, g % 2
    x, yh = t // NYH, t % NYH
    inner = yl + c == 1

    def mod(value, n):
        return lax.rem(value + n, n)

    right, left = (mod(z + 1, NZ) * 4 + yl * 2 + c, t), (mod(z - 1, NZ) * 4 + yl * 2 + c, t)
    beside = (z * 4 + (1 - yl) * 2 + c, t)
    across = (z * 4 + (1 - yl) * 2 + 1 - c, t)
    mate = (z * 4 + yl * 2 + 1 - c, t)
    x_peer = [None] + [(g, mod(x + k, NX) * NYH + yh) for k in range(1, NX)]
    y_peer = [None] + [(g, x * NYH + mod(yh + k, NYH)) for k in range(1, NYH)]

    third, rest = g // 12, g % 12
    perm_to = (12 * third + 4 * (rest % 3) + yh, x * NYH + rest // 3)
    perm_from = (12 * third + 3 * yh + rest // 4, x * NYH + g % 4)
    moves = jnp.logical_or(perm_to[0] != g, perm_to[1] != t)

    def place(head):
        return pl.multiple_of(((head % 2) * 2 + head // 2) * HD, HD)

    own = w.at[z, yl, c]
    load_w = pltpu.make_async_copy(win_hbm, own, local_sem.at[0])
    load_w.start()
    load_v = pltpu.make_async_copy(wout_hbm, piece, local_sem.at[1])
    load_v.start()
    load_l = pltpu.make_async_copy(lat_hbm, lat, local_sem.at[2])
    load_l.start()

    barrier = pltpu.get_barrier_semaphore()
    peers = [right, left, beside, across, mate] + x_peer[1:] + y_peer[1:]
    for peer in peers:
        pl.semaphore_signal(barrier, inc=1, device_id=peer, device_id_type=MESH)

    @pl.when(moves)
    def _():
        pl.semaphore_signal(barrier, inc=1, device_id=perm_to, device_id_type=MESH)
        pl.semaphore_signal(barrier, inc=1, device_id=perm_from, device_id_type=MESH)
        pl.semaphore_wait(barrier, len(peers) + 2)

    @pl.when(jnp.logical_not(moves))
    def _():
        pl.semaphore_wait(barrier, len(peers))

    def remote(src, dst, s, r, to):
        return pltpu.make_async_remote_copy(
            src_ref=src, dst_ref=dst, send_sem=s, recv_sem=r, device_id=to, device_id_type=MESH
        )

    def z_of(k):
        if k == 0:
            return z
        step = (k + 1) // 2
        return mod(z - step, NZ) if k % 2 == 1 else mod(z + step, NZ)

    class Ring:
        def __init__(self, quarter, pair, sems):
            self.quarter, self.pair = quarter, pair
            self.zs, self.zr, self.ys, self.yr, self.cs, self.cr = sems
            self.started = []

        def z_copy(self, way, step, landing):
            gone = step if landing else step - 1
            home = mod(z - gone, NZ) if way == 0 else mod(z + gone, NZ)
            ref = self.quarter(home, yl)
            if step == NZ // 2:
                half = ref.shape[0] // 2
                ref = ref.at[pl.ds(way * half, half)]
            return remote(
                ref, ref, self.zs.at[way, step - 1], self.zr.at[way, step - 1], right if way == 0 else left
            )

        def go(self, copy):
            copy.start()
            self.started.append(copy)

        def z_send(self, way, step):
            self.go(self.z_copy(way, step, False))

        def z_recv(self, way, step):
            self.z_copy(way, step, True).wait_recv()

        def y_copy(self, k, row):
            ref = self.quarter(z_of(k), row)
            return remote(ref, ref, self.ys.at[k], self.yr.at[k], beside)

        def y_send(self, k):
            self.go(self.y_copy(k, yl))

        def c_copy(self, k, core):
            ref = self.pair(z_of(k), core)
            return remote(ref, ref, self.cs.at[k], self.cr.at[k], mate)

        def first(self):
            self.z_send(0, 1)
            self.z_send(1, 1)
            self.y_send(0)

        def step(self, s):
            for way in range(2):
                self.z_recv(way, s)
                if s < NZ // 2:
                    self.z_send(way, s + 1)
                    self.y_send(2 * s - 1 + way)
            if s == NZ // 2:
                self.y_send(NZ - 1)

        def cross(self, s):
            for k in chunks_of(s):
                self.y_copy(k, 1 - yl).wait_recv()
                self.go(self.c_copy(k, c))

        def arrive(self, k):
            self.c_copy(k, 1 - c).wait_recv()

        def drain(self):
            for copy in self.started:
                copy.wait_send()

    ring = Ring(lambda h, row: w.at[h, row, c], lambda h, core: w.at[h, :, core], (wz_s, wz_r, wy_s, wy_r, wc_s, wc_r))

    def v_rows(h):
        return pl.ds(pl.multiple_of(h * RANK, RANK), RANK)

    ring2 = Ring(
        lambda h, row: w2.at[v_rows(h), pl.ds(pl.multiple_of(c * 256 + row * HD, HD), HD)],
        lambda h, core: w2.at[v_rows(h), pl.ds(pl.multiple_of(core * 256, 256), 256)],
        (vz_s, vz_r, vy_s, vy_r, vc_s, vc_r),
    )

    load_w.wait()
    ring.first()

    mine2 = w2.at[v_rows(z), pl.ds(pl.multiple_of(c * 256 + yl * HD, HD), HD)]
    perm = remote(piece, mine2, perm_sem.at[0], perm_sem.at[1], perm_to)
    keep = pltpu.make_async_copy(piece, mine2, local_sem.at[3])
    z_to, yl_to, c_to = perm_to[0] // 4, (perm_to[0] // 2) % 2, perm_to[0] % 2
    there = w2.at[v_rows(z_to), pl.ds(pl.multiple_of(c_to * 256 + yl_to * HD, HD), HD)]
    load_v.wait()

    @pl.when(moves)
    def _():
        remote(piece, there, perm_sem.at[0], perm_sem.at[1], perm_to).start()

    @pl.when(jnp.logical_not(moves))
    def _():
        keep.start()

    text_keys = rms(text[:, :HD].astype(F32), gains[1:2, :]).astype(BF16)
    slots = lax.broadcasted_iota(jnp.int32, (1, text.shape[0]), 1).astype(F32)
    text_bias = jnp.minimum(count[0].astype(F32) - 0.5 - slots, 0.0) * 1e30

    load_l.wait()

    def multiply(k):
        h = z_of(k)
        block = w[pl.ds(h, 1)].reshape(4 * RANK, 3 * HD)
        part_sum = jnp.dot(lat[:, pl.ds(pl.multiple_of(h * 256, 256), 256)], block, preferred_element_type=F32)
        if k == 0:
            acc[...] = part_sum
        else:
            acc[...] += part_sum

    steps = NZ // 2
    for s in range(1, steps + 1):
        ring.step(s)
        if s == 2:

            @pl.when(moves)
            def _():
                perm.wait()

            @pl.when(jnp.logical_not(moves))
            def _():
                keep.wait()

            ring2.first()
        if s >= 3:
            ring2.step(s - 2)
        ring.cross(s - 1)
        if s >= 2:
            for k in chunks_of(s - 2):
                ring.arrive(k)
                multiply(k)
    ring.cross(steps)
    for s in (steps - 1, steps):
        for k in chunks_of(s):
            ring.arrive(k)
            multiply(k)

    kv_started = []

    def kv_send(src, dst, s, r, to):
        remote(src, dst, s, r, to).start()

    def kv_mate(dt, p):
        return kv.at[dt, 1, p], kv.at[dt, 2 * c, p], kc_s.at[dt, p], kc_r.at[dt, p], mate

    def kv_across(dt, p):
        return kv.at[dt, 1, p], kv.at[dt, 2 * yl, p], ky_s.at[dt, p], ky_r.at[dt, p], across

    def kv_time(way, p):
        return kv.at[1, 1, p], kv.at[2 * way, 1, p], kz_s.at[way, p], kz_r.at[way, p], right if way == 0 else left

    later = [z < NZ - 1, z > 0]
    earlier = [z > 0, z < NZ - 1]

    def send_own(p):
        for way in range(2):

            @pl.when(later[way])
            def _(way=way):
                kv_send(*kv_time(way, p))

        @pl.when(inner)
        def _():
            kv_send(*kv_across(1, p))

        kv_send(*kv_mate(1, p))

    kv[1, 1, 0] = rms(acc[:, HD : 2 * HD], gains[1:2, :]).astype(BF16)
    send_own(0)
    kv[1, 1, 1] = acc[:, 2 * HD :].astype(BF16)
    send_own(1)
    ring2.step(5)
    scale = HD ** (-0.5) * 1.4426950408889634
    q[...] = (rms(acc[:, :HD], gains[0:1, :]) * scale).astype(BF16)

    def attend(keys, values, bias=None, start=False):
        for b in range(BLOCKS):
            rows = pl.ds(b * ROWS, ROWS)
            scores = lax.dot_general(q[rows, :], keys, NT, preferred_element_type=F32)
            if bias is not None:
                scores = scores + bias
            top = jnp.max(scores, axis=1, keepdims=True)
            if not start:
                before = m[rows, :1]
                top = jnp.maximum(before, top)
            weights = jnp.exp2(scores - top)
            total = jnp.sum(weights, axis=1, keepdims=True)
            mixed = jnp.dot(weights.astype(BF16), values, preferred_element_type=F32)
            if not start:
                fade = jnp.exp2(before - top)
                total = total + fade * l[rows, :1]
                mixed = mixed + fade * o[rows, :]
            m[rows, :] = jnp.broadcast_to(top, (ROWS, HD))
            l[rows, :] = jnp.broadcast_to(total, (ROWS, HD))
            o[rows, :] = mixed

    attend(text_keys, text[:, HD:], text_bias, start=True)
    attend(kv[1, 1, 0], kv[1, 1, 1])
    ring2.step(6)
    for s in range(steps + 1):
        ring2.cross(s)
    ring.drain()

    for p in range(2):
        for way in range(2):

            @pl.when(earlier[way])
            def _(way=way, p=p):
                ref = kv.at[2 * way, 1, p]
                remote(ref, ref, kz_s.at[way, p], kz_r.at[way, p], right).wait_recv()

                @pl.when(inner)
                def _():
                    kv_send(*kv_across(2 * way, p))

                kv_send(*kv_mate(2 * way, p))

    def take(dt, dh, s, r):
        for p in range(2):
            ref = kv.at[dt, dh, p]
            remote(ref, ref, s.at[dt, p], r.at[dt, p], mate).wait_recv()
        attend(kv[dt, dh, 0], kv[dt, dh, 1])

    from_mate, from_across = 2 - 2 * c, 2 - 2 * yl

    take(1, from_mate, kc_s, kc_r)
    for way in range(2):

        @pl.when(earlier[way])
        def _(way=way):
            attend(kv[2 * way, 1, 0], kv[2 * way, 1, 1])

    @pl.when(inner)
    def _():
        take(1, from_across, ky_s, ky_r)

    for way in range(2):

        @pl.when(earlier[way])
        def _(way=way):
            take(2 * way, from_mate, kc_s, kc_r)

    for k in range(NZ):
        ring2.arrive(k)
    ring2.drain()
    for way in range(2):

        @pl.when(jnp.logical_and(earlier[way], inner))
        def _(way=way):
            take(2 * way, from_across, ky_s, ky_r)

    def att_copy(b, k, head):
        ref = att.at[pl.ds(b * ROWS, ROWS), pl.ds(place(head), HD)]
        return remote(ref, ref, at_s.at[b, k - 1], at_r.at[b, k - 1], y_peer[k])

    def sum_copy(b, k):
        return remote(send.at[k - 1, b], got.at[k - 1, b], rs_s.at[b, k - 1], rs_r.at[b, k - 1], x_peer[k])

    for b in range(BLOCKS):
        rows = pl.ds(b * ROWS, ROWS)
        att[rows, pl.ds(place(yh), HD)] = (o[rows, :] / l[rows, :1]).astype(BF16)
        for k in range(1, NYH):
            att_copy(b, k, yh).start()

    for b in range(BLOCKS):
        for k in range(1, NYH):
            att_copy(b, k, mod(yh - k, NYH)).wait_recv()
        block = att[pl.ds(b * ROWS, ROWS), :]
        for k in (1, 2, 3, 0):
            rows = pl.ds(pl.multiple_of(mod(x + k, NX) * OUT, OUT), OUT)
            term = lax.dot_general(w2[rows, :], block, NT, preferred_element_type=F32)
            if k:
                send[k - 1, b] = term.astype(BF16)
                sum_copy(b, k).start()
            else:
                part[b] = term

    for b in range(BLOCKS):
        total = part[b]
        for k in range(1, NX):
            sum_copy(b, k).wait_recv()
            total = total + got[k - 1, b].astype(F32)
        out[:, pl.ds(b * ROWS, ROWS)] = total.astype(BF16)

    for p in range(2):
        for way in range(2):

            @pl.when(later[way])
            def _(way=way, p=p):
                remote(*kv_time(way, p)).wait_send()

        for dt in range(3):
            there_is = None if dt == 1 else earlier[dt // 2]

            def left_here(dt=dt, p=p):
                remote(*kv_mate(dt, p)).wait_send()

                @pl.when(inner)
                def _():
                    remote(*kv_across(dt, p)).wait_send()

            if there_is is None:
                left_here()
            else:
                pl.when(there_is)(left_here)
    for b in range(BLOCKS):
        for k in range(1, NX):
            sum_copy(b, k).wait_send()
            att_copy(b, k, yh).wait_send()


def local(latents, input_weight, norm_gains, text_pairs, text_count, output_weight):
    vmem, anywhere = pl.BlockSpec(memory_space=pltpu.VMEM), pl.BlockSpec(memory_space=pl.ANY)
    dma = pltpu.SemaphoreType.DMA
    steps = NZ // 2
    ring = [dma((2, steps)), dma((2, steps)), dma((NZ,)), dma((NZ,)), dma((NZ,)), dma((NZ,))]
    halo = [dma((2, 2)), dma((2, 2)), dma((3, 2)), dma((3, 2)), dma((3, 2)), dma((3, 2))]
    turned = pl.pallas_call(
        kernel,
        out_shape=jax.ShapeDtypeStruct((OUT, TILE), BF16),
        in_specs=[anywhere, anywhere, vmem, vmem, pl.BlockSpec(memory_space=pltpu.SMEM), anywhere],
        out_specs=vmem,
        scratch_shapes=[
            pltpu.VMEM((TILE, NZ * 4 * RANK), BF16),
            pltpu.VMEM((NZ, 2, 2, RANK, 3 * HD), BF16),
            pltpu.VMEM((NZ * RANK, NYH * HD), BF16),
            pltpu.VMEM((RANK, HD), BF16),
            pltpu.VMEM((TILE, 3 * HD), F32),
            pltpu.VMEM((TILE, HD), BF16),
            pltpu.VMEM((3, 3, 2, TILE, HD), BF16),
            pltpu.VMEM((TILE, HD), F32),
            pltpu.VMEM((TILE, HD), F32),
            pltpu.VMEM((TILE, HD), F32),
            pltpu.VMEM((TILE, NYH * HD), BF16),
            pltpu.VMEM((BLOCKS, OUT, ROWS), F32),
            pltpu.VMEM((NX - 1, BLOCKS, OUT, ROWS), BF16),
            pltpu.VMEM((NX - 1, BLOCKS, OUT, ROWS), BF16),
            dma((4,)),
            dma((2,)),
            *ring,
            *ring,
            *halo,
            dma((BLOCKS, NYH - 1)),
            dma((BLOCKS, NYH - 1)),
            dma((BLOCKS, NX - 1)),
            dma((BLOCKS, NX - 1)),
        ],
        compiler_params=pltpu.CompilerParams(
            collective_id=0, has_side_effects=True, vmem_limit_bytes=60 * 1024 * 1024
        ),
        name="sublayer",
    )(latents, input_weight, norm_gains, text_pairs, text_count, output_weight.T)
    return turned.T


def solution(mesh):
    placed = (P("grid", None), P("grid", "tp"), P(), P(None, "tp"), P(), P("tp", "grid"))
    return jax.shard_map(
        local, mesh=mesh, in_specs=placed, out_specs=P("grid", "tp"), check_vma=False
    )
```

time: 282 us -> 77.7 us (0.28)
  the two profiles are of different devices: /device:TPU:6 before, /device:TPU:72 now
where the time goes in v1:
time: 77.7 us; the launch traced here: 77.5 us
  Pallas kernels  75.2 us (97%)
  local copies, waits for them, and re-layouts  1.59 us (2%)
    pallas_call x1, Pallas kernels, local(): pl.pallas_call(kernel, out_shape=jax.ShapeDtypeStruct((OUT, TILE), BF16),...  75.2 us
    unnamed x1, local copies, waits for them, and re-layouts  1.59 us

profile of v1, /device:TPU:72, one launch (start us, length us, event | category | flops | bytes accessed | tf_op | source)
XLA Modules:
  0.0 77.5 jit_solution(1208735759978513947)
XLA Ops:
  0.7 75.2 %sublayer.1 = bf16[192,384]{1,0:T(8,128)(2,1)} custom-call(bf16[384,3072]{1,0:T(8,128)(2,1)} %lat_hbm.1, bf16[64,384]{1,0:T(8,128)(2,1)} %win_hbm.1, f32[2,128]{1,0:T(2,128)} %gains.1, bf16[256,256]{1,0:T(8,128)(2,1)} %text.1, s32[1]{0:T(128)S(6)} %copy.8.count, bf16[64,128]{1,0:T(8,128)(2,1)} %bitcast.3), custom_call_target="tpu_custom_call" | custom-call | tf_op jit(solution)/shard_map/sublayer/pallas_call | solution.py:420
  75.9 1.6 %copy.9 = bf16[384,192]{0,1:T(8,128)(2,1)} copy(bf16[384,192]{0,1:T(8,128)(2,1)} %bitcast.2) | data formatting | bytes 294912

commit v2 on v1

v2 whole, which is shorter than its diff:
```python
import functools

import jax
import jax.numpy as jnp
from jax import lax
from jax.experimental import pallas as pl
from jax.experimental.pallas import tpu as pltpu
from jax.sharding import PartitionSpec as P

NZ = 12
NX = 4
NYH = 4
TILE = 384
HD = 128
RANK = 64
BLOCKS = 3
ROWS = TILE // BLOCKS
OUT = 192
EPS = 1e-6
MESH = pl.DeviceIdType.MESH
F32 = jnp.float32
BF16 = jnp.bfloat16


def rms(values, gain):
    return values * lax.rsqrt(jnp.mean(values * values, axis=-1, keepdims=True) + EPS) * gain


ORDER = [0, 2, -2, 1, -1, 4, -4, 3, -3, 5, -5, 6]
PARENT = {1: 0, 2: 0, 3: 2, 4: 2, 5: 4, 6: 4}
EDGES = [2, -2, 1, -1, 4, -4, 3, -3, 5, -5, 6, -6]


def parent(offset):
    return PARENT[offset] if offset > 0 else -PARENT[-offset]


def kernel(
    lat_hbm, win_hbm, gains, text, count, wout_hbm, out,
    lat, w, w2, piece, acc, q, kb, vb, m, l, o, att, part, send, got,
    local_sem, perm_sem,
    wz_s, wz_r, wy_s, wy_r, wc_s, wc_r,
    vz_s, vz_r, v_sem,
    kz_s, kz_r, ky_s, ky_r, kc_s, kc_r,
    at_s, at_r, rs_s, rs_r,
):
    g = lax.axis_index("grid")
    t = lax.axis_index("tp")
    z, yl, c = g // 4, (g // 2) % 2, g % 2
    x, yh = t // NYH, t % NYH
    inner = yl + c == 1

    def mod(value, n):
        return lax.rem(value + n, n)

    z_peer = {k: (mod(z + k, NZ) * 4 + yl * 2 + c, t) for k in (1, -1, 2, -2)}
    slant = [(mod(z + k, NZ) * 4 + (1 - yl) * 2 + 1 - c, t) for k in (1, -1)]
    beside = (z * 4 + (1 - yl) * 2 + c, t)
    across = (z * 4 + (1 - yl) * 2 + 1 - c, t)
    mate = (z * 4 + yl * 2 + 1 - c, t)
    x_peer = [None] + [(g, mod(x + k, NX) * NYH + yh) for k in range(1, NX)]
    y_peer = [None] + [(g, x * NYH + mod(yh + k, NYH)) for k in range(1, NYH)]

    third, rest = g // 12, g % 12
    perm_to = (12 * third + 4 * (rest % 3) + yh, x * NYH + rest // 3)
    perm_from = (12 * third + 3 * yh + rest // 4, x * NYH + g % 4)
    moves = jnp.logical_or(perm_to[0] != g, perm_to[1] != t)

    def place(head):
        return (head % 2) * 2 + head // 2

    own = w.at[z, yl, c]
    load_w = pltpu.make_async_copy(win_hbm, own, local_sem.at[0])
    load_w.start()
    load_v = pltpu.make_async_copy(wout_hbm, piece, local_sem.at[1])
    load_v.start()
    load_l = pltpu.make_async_copy(lat_hbm, lat, local_sem.at[2])
    load_l.start()

    barrier = pltpu.get_barrier_semaphore()
    peers = list(z_peer.values()) + slant + [beside, across, mate] + x_peer[1:] + y_peer[1:]
    for peer in peers:
        pl.semaphore_signal(barrier, inc=1, device_id=peer, device_id_type=MESH)

    @pl.when(moves)
    def _():
        pl.semaphore_signal(barrier, inc=1, device_id=perm_to, device_id_type=MESH)
        pl.semaphore_signal(barrier, inc=1, device_id=perm_from, device_id_type=MESH)
        pl.semaphore_wait(barrier, len(peers) + 2)

    @pl.when(jnp.logical_not(moves))
    def _():
        pl.semaphore_wait(barrier, len(peers))

    def remote(src, dst, s, r, to):
        return pltpu.make_async_remote_copy(
            src_ref=src, dst_ref=dst, send_sem=s, recv_sem=r, device_id=to, device_id_type=MESH
        )

    class Ring:
        def __init__(self, quarter, pair, sems):
            self.quarter, self.pair = quarter, pair
            self.zs, self.zr = sems[:2]
            if pair:
                self.ys, self.yr, self.cs, self.cr = sems[2:]
            self.started = []

        def go(self, copy):
            copy.start()
            self.started.append(copy)

        def z_copy(self, offset, landing):
            at = offset if landing else parent(offset)
            ref = self.quarter(mod(z - at, NZ), yl)
            if abs(offset) == NZ // 2:
                half = ref.shape[0] // 2
                ref = ref.at[pl.ds(half if offset < 0 else 0, half)]
            e = EDGES.index(offset)
            return remote(ref, ref, self.zs.at[e], self.zr.at[e], z_peer[offset - parent(offset)])

        def z_recv(self, offset):
            self.z_copy(offset, True).wait_recv()

        def z_forward(self, at):
            for offset in EDGES:
                if parent(offset) == at and (at or offset) and (at * offset > 0 or at == 0):
                    self.go(self.z_copy(offset, False))

        def y_copy(self, offset, row):
            ref = self.quarter(mod(z - offset, NZ), row)
            e = ORDER.index(offset)
            return remote(ref, ref, self.ys.at[e], self.yr.at[e], beside)

        def c_copy(self, offset, core):
            ref = self.pair(mod(z - offset, NZ), core)
            e = ORDER.index(offset)
            return remote(ref, ref, self.cs.at[e], self.cr.at[e], mate)

        def first(self):
            self.z_forward(0)
            if self.pair:
                self.go(self.y_copy(0, yl))

        def take(self, offset):
            self.z_recv(offset)
            if offset == NZ // 2:
                self.z_recv(-offset)
            self.z_forward(offset)
            if self.pair:
                self.go(self.y_copy(offset, yl))

        def cross(self, offset):
            self.y_copy(offset, 1 - yl).wait_recv()
            self.go(self.c_copy(offset, c))

        def arrive(self, offset):
            self.c_copy(offset, 1 - c).wait_recv()

        def drain(self):
            for copy in self.started:
                copy.wait_send()

    ring = Ring(lambda h, row: w.at[h, row, c], lambda h, core: w.at[h, :, core], (wz_s, wz_r, wy_s, wy_r, wc_s, wc_r))

    def v_rows(h):
        return pl.ds(pl.multiple_of(h * RANK, RANK), RANK)

    ring2 = Ring(lambda h, row: w2.at[2 * c + row, v_rows(h)], None, (vz_s, vz_r))

    def w2_beside(row):
        return remote(w2.at[2 * c + row], w2.at[2 * c + row], v_sem.at[0], v_sem.at[1], beside)

    def w2_mate(core):
        ref = w2.at[pl.ds(2 * core, 2)]
        return remote(ref, ref, v_sem.at[2], v_sem.at[3], mate)

    load_w.wait()
    ring.first()

    mine2 = w2.at[2 * c + yl, v_rows(z)]
    perm = remote(piece, mine2, perm_sem.at[0], perm_sem.at[1], perm_to)
    keep = pltpu.make_async_copy(piece, mine2, local_sem.at[3])
    z_to, yl_to, c_to = perm_to[0] // 4, (perm_to[0] // 2) % 2, perm_to[0] % 2
    there = w2.at[2 * c_to + yl_to, v_rows(z_to)]
    load_v.wait()

    @pl.when(moves)
    def _():
        remote(piece, there, perm_sem.at[0], perm_sem.at[1], perm_to).start()

    @pl.when(jnp.logical_not(moves))
    def _():
        keep.start()

    text_keys = rms(text[:, :HD].astype(F32), gains[1:2, :]).astype(BF16)
    text_values = text[:, HD:].astype(F32).T.astype(BF16)
    slots = lax.broadcasted_iota(jnp.int32, (text.shape[0], 1), 0).astype(F32)
    text_bias = jnp.minimum(count[0].astype(F32) - 0.5 - slots, 0.0) * 1e30

    load_l.wait()

    def multiply(offset):
        h = mod(z - offset, NZ)
        block = w[pl.ds(h, 1)].reshape(4 * RANK, 3 * HD)
        part_sum = jnp.dot(lat[:, pl.ds(pl.multiple_of(h * 256, 256), 256)], block, preferred_element_type=F32)
        if offset == 0:
            acc[...] = part_sum
        else:
            acc[...] += part_sum

    def project(offsets):
        for offset in offsets:
            ring.arrive(offset)
            multiply(offset)

    first, second, third_ = ORDER[1:5], ORDER[5:9], ORDER[9:]
    for offset in first:
        ring.take(offset)
    ring.cross(0)

    @pl.when(moves)
    def _():
        perm.wait()

    @pl.when(jnp.logical_not(moves))
    def _():
        keep.wait()

    ring2.first()
    for offset in second:
        ring.take(offset)
    for offset in first:
        ring2.take(offset)
    for offset in first:
        ring.cross(offset)
    project([0])
    for offset in third_:
        ring.take(offset)
    for offset in second:
        ring2.take(offset)
    for offset in second:
        ring.cross(offset)
    project(first)
    for offset in third_:
        ring.cross(offset)
    project(second)
    project(third_)

    kv_started = []

    def kv_send(src, dst, s, r, to):
        remote(src, dst, s, r, to).start()

    def slot(dt, dh, p):
        return (vb if p else kb).at[dt, dh]

    def kv_mate(dt, p):
        return slot(dt, 1, p), slot(dt, 2 * c, p), kc_s.at[dt, p], kc_r.at[dt, p], mate

    def kv_across(p):
        return slot(1, 1, p), slot(1, 2 * yl, p), ky_s.at[1, p], ky_r.at[1, p], across

    def kv_slant(way, p):
        return slot(1, 1, p), slot(2 * way, 2 * yl, p), ky_s.at[2 * way, p], ky_r.at[2 * way, p], slant[way]

    def kv_time(way, p):
        return slot(1, 1, p), slot(2 * way, 1, p), kz_s.at[way, p], kz_r.at[way, p], z_peer[1 - 2 * way]

    later = [z < NZ - 1, z > 0]
    earlier = [z > 0, z < NZ - 1]

    def send_own(p):
        for way in range(2):

            @pl.when(later[way])
            def _(way=way):
                kv_send(*kv_time(way, p))

        @pl.when(inner)
        def _():
            kv_send(*kv_across(p))

        for way in range(2):

            @pl.when(jnp.logical_and(later[way], inner))
            def _(way=way):
                kv_send(*kv_slant(way, p))

        kv_send(*kv_mate(1, p))

    kb[1, 1] = rms(acc[:, HD : 2 * HD], gains[1:2, :]).astype(BF16)
    send_own(0)
    vb[1, 1] = acc[:, 2 * HD :].T.astype(BF16)
    send_own(1)
    scale = HD ** (-0.5) * 1.4426950408889634
    q[...] = (rms(acc[:, :HD], gains[0:1, :]) * scale).T.astype(BF16)

    def attend(keys, values, bias=None, start=False):
        scores = jnp.dot(keys, q[...], preferred_element_type=F32)
        if bias is not None:
            scores = scores + bias
        top = jnp.max(scores, axis=0, keepdims=True)
        if not start:
            before = m[...]
            top = jnp.maximum(before, top)
        weights = jnp.exp2(scores - top)
        total = jnp.sum(weights, axis=0, keepdims=True)
        mixed = jnp.dot(values, weights.astype(BF16), preferred_element_type=F32)
        if not start:
            fade = jnp.exp2(before - top)
            total = total + fade * l[...]
            mixed = mixed + fade * o[...]
        m[...] = top
        l[...] = total
        o[...] = mixed

    def attend_tile(dt, dh):
        attend(kb[dt, dh], vb[dt, dh])

    attend(text_keys, text_values, text_bias, start=True)
    for offset in third_:
        ring2.take(offset)
    w2_beside(yl).start()
    attend_tile(1, 1)

    for p in range(2):
        for way in range(2):

            @pl.when(earlier[way])
            def _(way=way, p=p):
                ref = slot(2 * way, 1, p)
                remote(ref, ref, kz_s.at[way, p], kz_r.at[way, p], mate).wait_recv()
                kv_send(*kv_mate(2 * way, p))

    def land(dt, dh, s, r):
        for p in range(2):
            ref = slot(dt, dh, p)
            remote(ref, ref, s.at[dt, p], r.at[dt, p], mate).wait_recv()

    from_mate, from_across = 2 - 2 * c, 2 - 2 * yl

    land(1, from_mate, kc_s, kc_r)
    attend_tile(1, from_mate)
    for way in range(2):

        @pl.when(earlier[way])
        def _(way=way):
            attend_tile(2 * way, 1)

    w2_beside(1 - yl).wait_recv()
    w2_mate(c).start()

    @pl.when(inner)
    def _():
        land(1, from_across, ky_s, ky_r)
        attend_tile(1, from_across)

    for way in range(2):

        @pl.when(earlier[way])
        def _(way=way):
            land(2 * way, from_mate, kc_s, kc_r)
            attend_tile(2 * way, from_mate)

    for way in range(2):

        @pl.when(jnp.logical_and(earlier[way], inner))
        def _(way=way):
            land(2 * way, from_across, ky_s, ky_r)
            attend_tile(2 * way, from_across)

    def halo_drain():
        for p in range(2):
            remote(*kv_mate(1, p)).wait_send()

            @pl.when(inner)
            def _(p=p):
                remote(*kv_across(p)).wait_send()

            for way in range(2):

                @pl.when(later[way])
                def _(way=way, p=p):
                    remote(*kv_time(way, p)).wait_send()

                @pl.when(jnp.logical_and(later[way], inner))
                def _(way=way, p=p):
                    remote(*kv_slant(way, p)).wait_send()

                @pl.when(earlier[way])
                def _(way=way, p=p):
                    remote(*kv_mate(2 * way, p)).wait_send()

    def att_copy(b, k, head):
        ref = att.at[b, place(head)]
        return remote(ref, ref, at_s.at[b, k - 1], at_r.at[b, k - 1], y_peer[k])

    def sum_copy(b, k):
        return remote(send.at[k - 1, b], got.at[k - 1, b], rs_s.at[b, k - 1], rs_r.at[b, k - 1], x_peer[k])

    turn = 1.0 / l[...]
    for b in range(BLOCKS):
        rows = pl.ds(b * ROWS, ROWS)
        att[b, place(yh)] = (o[:, rows] * turn[:, b * ROWS : (b + 1) * ROWS]).astype(BF16)
        for k in range(1, NYH):
            att_copy(b, k, yh).start()
    ring.drain()
    ring2.drain()
    w2_beside(yl).wait_send()
    w2_mate(1 - c).wait_recv()
    w2_mate(c).wait_send()
    halo_drain()

    for b in range(BLOCKS):
        for k in range(1, NYH):
            att_copy(b, k, mod(yh - k, NYH)).wait_recv()
        block = att[b].reshape(NYH * HD, ROWS)
        for k in (1, 2, 3, 0):
            rows = pl.ds(pl.multiple_of(mod(x + k, NX) * OUT, OUT), OUT)
            weight = jnp.concatenate([w2[p, rows, :] for p in range(NYH)], axis=1)
            term = jnp.dot(weight, block, preferred_element_type=F32)
            if k:
                send[k - 1, b] = term.astype(BF16)
                sum_copy(b, k).start()
            else:
                part[b] = term

    for b in range(BLOCKS):
        for k in range(1, NYH):
            att_copy(b, k, yh).wait_send()
    for b in range(BLOCKS):
        total = part[b]
        for k in range(1, NX):
            sum_copy(b, k).wait_recv()
            total = total + got[k - 1, b].astype(F32)
        out[:, pl.ds(b * ROWS, ROWS)] = total.astype(BF16)

    for b in range(BLOCKS):
        for k in range(1, NX):
            sum_copy(b, k).wait_send()


def local(latents, input_weight, norm_gains, text_pairs, text_count, output_weight):
    vmem, anywhere = pl.BlockSpec(memory_space=pltpu.VMEM), pl.BlockSpec(memory_space=pl.ANY)
    dma = pltpu.SemaphoreType.DMA
    ring = [dma((NZ,)), dma((NZ,)), dma((NZ,)), dma((NZ,)), dma((NZ,)), dma((NZ,))]
    halo = [dma((2, 2)), dma((2, 2)), dma((3, 2)), dma((3, 2)), dma((3, 2)), dma((3, 2))]
    turned = pl.pallas_call(
        kernel,
        out_shape=jax.ShapeDtypeStruct((OUT, TILE), BF16),
        in_specs=[anywhere, anywhere, vmem, vmem, pl.BlockSpec(memory_space=pltpu.SMEM), anywhere],
        out_specs=vmem,
        scratch_shapes=[
            pltpu.VMEM((TILE, NZ * 4 * RANK), BF16),
            pltpu.VMEM((NZ, 2, 2, RANK, 3 * HD), BF16),
            pltpu.VMEM((NYH, NZ * RANK, HD), BF16),
            pltpu.VMEM((RANK, HD), BF16),
            pltpu.VMEM((TILE, 3 * HD), F32),
            pltpu.VMEM((HD, TILE), BF16),
            pltpu.VMEM((3, 3, TILE, HD), BF16),
            pltpu.VMEM((3, 3, HD, TILE), BF16),
            pltpu.VMEM((1, TILE), F32),
            pltpu.VMEM((1, TILE), F32),
            pltpu.VMEM((HD, TILE), F32),
            pltpu.VMEM((BLOCKS, NYH, HD, ROWS), BF16),
            pltpu.VMEM((BLOCKS, OUT, ROWS), F32),
            pltpu.VMEM((NX - 1, BLOCKS, OUT, ROWS), BF16),
            pltpu.VMEM((NX - 1, BLOCKS, OUT, ROWS), BF16),
            dma((4,)),
            dma((2,)),
            *ring,
            dma((NZ,)),
            dma((NZ,)),
            dma((4,)),
            *halo,
            dma((BLOCKS, NYH - 1)),
            dma((BLOCKS, NYH - 1)),
            dma((BLOCKS, NX - 1)),
            dma((BLOCKS, NX - 1)),
        ],
        compiler_params=pltpu.CompilerParams(
            collective_id=0, has_side_effects=True, vmem_limit_bytes=60 * 1024 * 1024
        ),
        name="sublayer",
    )(latents, input_weight, norm_gains, text_pairs, text_count, output_weight.T)
    return turned.T


def solution(mesh):
    placed = (P("grid", None), P("grid", "tp"), P(), P(None, "tp"), P(), P("tp", "grid"))
    return jax.shard_map(
        local, mesh=mesh, in_specs=placed, out_specs=P("grid", "tp"), check_vma=False
    )
```

time: 77.7 us -> 72.5 us (0.933)
  the two profiles are of different devices: /device:TPU:72 before, /device:TPU:64 now
where the time goes in v2:
time: 72.5 us; the launch traced here: 72.3 us
  Pallas kernels  70.1 us (97%)
  local copies, waits for them, and re-layouts  1.59 us (2%)
    pallas_call x1, Pallas kernels, local(): pl.pallas_call(kernel, out_shape=jax.ShapeDtypeStruct((OUT, TILE), BF16),...  70.1 us
    unnamed x1, local copies, waits for them, and re-layouts  1.59 us

profile of v2, /device:TPU:64, one launch (start us, length us, event | category | flops | bytes accessed | tf_op | source)
XLA Modules:
  0.0 72.3 jit_solution(10767446354371885475)
XLA Ops:
  0.7 70.1 %sublayer.1 = bf16[192,384]{1,0:T(8,128)(2,1)} custom-call(bf16[384,3072]{1,0:T(8,128)(2,1)} %lat_hbm.1, bf16[64,384]{1,0:T(8,128)(2,1)} %win_hbm.1, f32[2,128]{1,0:T(2,128)} %gains.1, bf16[256,256]{1,0:T(8,128)(2,1)} %text.1, s32[1]{0:T(128)S(6)} %copy.8.count, bf16[64,128]{1,0:T(8,128)(2,1)} %bitcast.3), custom_call_target="tpu_custom_call" | custom-call | tf_op jit(solution)/shard_map/sublayer/pallas_call | solution.py:448
  70.7 1.6 %copy.9 = bf16[384,192]{0,1:T(8,128)(2,1)} copy(bf16[384,192]{0,1:T(8,128)(2,1)} %bitcast.2) | data formatting | bytes 294912

commit v3 on v2

--- a/solution.py
+++ b/solution.py
@@ -218,31 +218,32 @@
         ring.take(offset)
     ring.cross(0)
 
-    @pl.when(moves)
-    def _():
-        perm.wait()
-
-    @pl.when(jnp.logical_not(moves))
-    def _():
-        keep.wait()
-
-    ring2.first()
     for offset in second:
         ring.take(offset)
-    for offset in first:
-        ring2.take(offset)
+
+    @pl.when(moves)
+    def _():
+        perm.wait()
+
+    @pl.when(jnp.logical_not(moves))
+    def _():
+        keep.wait()
+
+    ring2.first()
     for offset in first:
         ring.cross(offset)
     project([0])
     for offset in third_:
         ring.take(offset)
-    for offset in second:
+    for offset in first:
         ring2.take(offset)
     for offset in second:
         ring.cross(offset)
     project(first)
     for offset in third_:
         ring.cross(offset)
+    for offset in second:
+        ring2.take(offset)
     project(second)
     project(third_)
 
@@ -279,12 +280,6 @@
         @pl.when(inner)
         def _():
             kv_send(*kv_across(p))
-
-        for way in range(2):
-
-            @pl.when(jnp.logical_and(later[way], inner))
-            def _(way=way):
-                kv_send(*kv_slant(way, p))
 
         kv_send(*kv_mate(1, p))
 
@@ -295,29 +290,36 @@
     scale = HD ** (-0.5) * 1.4426950408889634
     q[...] = (rms(acc[:, :HD], gains[0:1, :]) * scale).T.astype(BF16)
 
-    def attend(keys, values, bias=None, start=False):
-        scores = jnp.dot(keys, q[...], preferred_element_type=F32)
+    def attend(keys, values, bias=None, start=False, at=slice(None)):
+        scores = jnp.dot(keys, q[:, at], preferred_element_type=F32)
         if bias is not None:
             scores = scores + bias
         top = jnp.max(scores, axis=0, keepdims=True)
         if not start:
-            before = m[...]
+            before = m[:, at]
             top = jnp.maximum(before, top)
         weights = jnp.exp2(scores - top)
         total = jnp.sum(weights, axis=0, keepdims=True)
         mixed = jnp.dot(values, weights.astype(BF16), preferred_element_type=F32)
         if not start:
             fade = jnp.exp2(before - top)
-            total = total + fade * l[...]
-            mixed = mixed + fade * o[...]
-        m[...] = top
-        l[...] = total
-        o[...] = mixed
-
-    def attend_tile(dt, dh):
-        attend(kb[dt, dh], vb[dt, dh])
+            total = total + fade * l[:, at]
+            mixed = mixed + fade * o[:, at]
+        m[:, at] = top
+        l[:, at] = total
+        o[:, at] = mixed
+
+    def attend_tile(dt, dh, at=slice(None)):
+        attend(kb[dt, dh], vb[dt, dh], at=at)
 
     attend(text_keys, text_values, text_bias, start=True)
+    for p in range(2):
+        for way in range(2):
+
+            @pl.when(jnp.logical_and(later[way], inner))
+            def _(way=way, p=p):
+                kv_send(*kv_slant(way, p))
+
     for offset in third_:
         ring2.take(offset)
     w2_beside(yl).start()
@@ -367,7 +369,6 @@
         @pl.when(jnp.logical_and(earlier[way], inner))
         def _(way=way):
             land(2 * way, from_across, ky_s, ky_r)
-            attend_tile(2 * way, from_across)
 
     def halo_drain():
         for p in range(2):
@@ -398,10 +399,15 @@
     def sum_copy(b, k):
         return remote(send.at[k - 1, b], got.at[k - 1, b], rs_s.at[b, k - 1], rs_r.at[b, k - 1], x_peer[k])
 
-    turn = 1.0 / l[...]
     for b in range(BLOCKS):
         rows = pl.ds(b * ROWS, ROWS)
-        att[b, place(yh)] = (o[:, rows] * turn[:, b * ROWS : (b + 1) * ROWS]).astype(BF16)
+        for way in range(2):
+
+            @pl.when(jnp.logical_and(earlier[way], inner))
+            def _(way=way, rows=rows):
+                attend_tile(2 * way, from_across, rows)
+
+        att[b, place(yh)] = (o[:, rows] * (1.0 / l[:, rows])).astype(BF16)
         for k in range(1, NYH):
             att_copy(b, k, yh).start()
     ring.drain()
@@ -415,7 +421,7 @@
         for k in range(1, NYH):
             att_copy(b, k, mod(yh - k, NYH)).wait_recv()
         block = att[b].reshape(NYH * HD, ROWS)
-        for k in (1, 2, 3, 0):
+        for k in (2, 1, 3, 0):
             rows = pl.ds(pl.multiple_of(mod(x + k, NX) * OUT, OUT), OUT)
             weight = jnp.concatenate([w2[p, rows, :] for p in range(NYH)], axis=1)
             term = jnp.dot(weight, block, preferred_element_type=F32)

time: 72.5 us -> 72 us (level)
  no operation moved by 1% of the time
where the time goes in v3:
time: 72 us; the launch traced here: 71.7 us
  Pallas kernels  69.5 us (97%)
  local copies, waits for them, and re-layouts  1.59 us (2%)
    pallas_call x1, Pallas kernels, local(): pl.pallas_call(kernel, out_shape=jax.ShapeDtypeStruct((OUT, TILE), BF16),...  69.5 us
    unnamed x1, local copies, waits for them, and re-layouts  1.59 us

profile of v3, /device:TPU:64, one launch (start us, length us, event | category | flops | bytes accessed | tf_op | source)
XLA Modules:
  0.0 71.7 jit_solution(16407214918903727718)
XLA Ops:
  0.7 69.5 %sublayer.1 = bf16[192,384]{1,0:T(8,128)(2,1)} custom-call(bf16[384,3072]{1,0:T(8,128)(2,1)} %lat_hbm.1, bf16[64,384]{1,0:T(8,128)(2,1)} %win_hbm.1, f32[2,128]{1,0:T(2,128)} %gains.1, bf16[256,256]{1,0:T(8,128)(2,1)} %text.1, s32[1]{0:T(128)S(6)} %copy.8.count, bf16[64,128]{1,0:T(8,128)(2,1)} %bitcast.3), custom_call_target="tpu_custom_call" | custom-call | tf_op jit(solution)/shard_map/sublayer/pallas_call | solution.py:454
  70.1 1.6 %copy.9 = bf16[384,192]{0,1:T(8,128)(2,1)} copy(bf16[384,192]{0,1:T(8,128)(2,1)} %bitcast.2) | data formatting | bytes 294912

commit v4 on v3

--- a/solution.py
+++ b/solution.py
@@ -290,29 +290,41 @@
     scale = HD ** (-0.5) * 1.4426950408889634
     q[...] = (rms(acc[:, :HD], gains[0:1, :]) * scale).T.astype(BF16)
 
-    def attend(keys, values, bias=None, start=False, at=slice(None)):
-        scores = jnp.dot(keys, q[:, at], preferred_element_type=F32)
-        if bias is not None:
-            scores = scores + bias
-        top = jnp.max(scores, axis=0, keepdims=True)
+    def attend(tiles, start=False):
+        scores = []
+        for keys, _, bias in tiles:
+            these = jnp.dot(keys, q[...], preferred_element_type=F32)
+            scores.append(these if bias is None else these + bias)
+        tops = [jnp.max(these, axis=0, keepdims=True) for these in scores]
         if not start:
-            before = m[:, at]
-            top = jnp.maximum(before, top)
-        weights = jnp.exp2(scores - top)
-        total = jnp.sum(weights, axis=0, keepdims=True)
-        mixed = jnp.dot(values, weights.astype(BF16), preferred_element_type=F32)
+            tops.append(m[...])
+        top = functools.reduce(jnp.maximum, tops)
         if not start:
-            fade = jnp.exp2(before - top)
-            total = total + fade * l[:, at]
-            mixed = mixed + fade * o[:, at]
-        m[:, at] = top
-        l[:, at] = total
-        o[:, at] = mixed
-
-    def attend_tile(dt, dh, at=slice(None)):
-        attend(kb[dt, dh], vb[dt, dh], at=at)
-
-    attend(text_keys, text_values, text_bias, start=True)
+            fade = jnp.exp2(m[...] - top)
+            total, mixed = fade * l[...], fade * o[...]
+        else:
+            total, mixed = 0.0, 0.0
+        for these, (_, values, _) in zip(scores, tiles):
+            weights = jnp.exp2(these - top)
+            total = total + jnp.sum(weights, axis=0, keepdims=True)
+            mixed = mixed + jnp.dot(values, weights.astype(BF16), preferred_element_type=F32)
+        m[...] = top
+        l[...] = total
+        o[...] = mixed
+
+    def tile(dt, dh):
+        return kb[dt, dh], vb[dt, dh], None
+
+    def attend_times(dh, where=None):
+        both = jnp.logical_and(earlier[0], earlier[1])
+        cases = [(both, (0, 2))] + [(jnp.logical_not(earlier[1 - way]), (2 * way,)) for way in range(2)]
+        for case, times in cases:
+
+            @pl.when(case if where is None else jnp.logical_and(case, where))
+            def _(times=times):
+                attend([tile(dt, dh) for dt in times])
+
+    attend([(text_keys, text_values, text_bias), tile(1, 1)], start=True)
     for p in range(2):
         for way in range(2):
 
@@ -323,7 +335,16 @@
     for offset in third_:
         ring2.take(offset)
     w2_beside(yl).start()
-    attend_tile(1, 1)
+
+    def land(dt, dh, s, r):
+        for p in range(2):
+            ref = slot(dt, dh, p)
+            remote(ref, ref, s.at[dt, p], r.at[dt, p], mate).wait_recv()
+
+    from_mate, from_across = 2 - 2 * c, 2 - 2 * yl
+
+    land(1, from_mate, kc_s, kc_r)
+    attend([tile(1, from_mate)])
 
     for p in range(2):
         for way in range(2):
@@ -334,35 +355,22 @@
                 remote(ref, ref, kz_s.at[way, p], kz_r.at[way, p], mate).wait_recv()
                 kv_send(*kv_mate(2 * way, p))
 
-    def land(dt, dh, s, r):
-        for p in range(2):
-            ref = slot(dt, dh, p)
-            remote(ref, ref, s.at[dt, p], r.at[dt, p], mate).wait_recv()
-
-    from_mate, from_across = 2 - 2 * c, 2 - 2 * yl
-
-    land(1, from_mate, kc_s, kc_r)
-    attend_tile(1, from_mate)
-    for way in range(2):
-
-        @pl.when(earlier[way])
-        def _(way=way):
-            attend_tile(2 * way, 1)
-
+    attend_times(1)
     w2_beside(1 - yl).wait_recv()
     w2_mate(c).start()
 
     @pl.when(inner)
     def _():
         land(1, from_across, ky_s, ky_r)
-        attend_tile(1, from_across)
+        attend([tile(1, from_across)])
 
     for way in range(2):
 
         @pl.when(earlier[way])
         def _(way=way):
             land(2 * way, from_mate, kc_s, kc_r)
-            attend_tile(2 * way, from_mate)
+
+    attend_times(from_mate)
 
     for way in range(2):
 
@@ -370,6 +378,8 @@
         def _(way=way):
             land(2 * way, from_across, ky_s, ky_r)
 
+    attend_times(from_across, inner)
+
     def halo_drain():
         for p in range(2):
             remote(*kv_mate(1, p)).wait_send()
@@ -401,12 +411,6 @@
 
     for b in range(BLOCKS):
         rows = pl.ds(b * ROWS, ROWS)
-        for way in range(2):
-
-            @pl.when(jnp.logical_and(earlier[way], inner))
-            def _(way=way, rows=rows):
-                attend_tile(2 * way, from_across, rows)
-
         att[b, place(yh)] = (o[:, rows] * (1.0 / l[:, rows])).astype(BF16)
         for k in range(1, NYH):
             att_copy(b, k, yh).start()

time: 72 us -> 71.6 us (level)
  no operation moved by 1% of the time
where the time goes in v4:
time: 71.6 us; the launch traced here: 71.4 us
  Pallas kernels  69.1 us (97%)
  local copies, waits for them, and re-layouts  1.59 us (2%)
    pallas_call x1, Pallas kernels, local(): pl.pallas_call(kernel, out_shape=jax.ShapeDtypeStruct((OUT, TILE), BF16),...  69.1 us
    unnamed x1, local copies, waits for them, and re-layouts  1.59 us

profile of v4, /device:TPU:64, one launch (start us, length us, event | category | flops | bytes accessed | tf_op | source)
XLA Modules:
  0.0 71.4 jit_solution(11738911288202400147)
XLA Ops:
  0.7 69.1 %sublayer.1 = bf16[192,384]{1,0:T(8,128)(2,1)} custom-call(bf16[384,3072]{1,0:T(8,128)(2,1)} %lat_hbm.1, bf16[64,384]{1,0:T(8,128)(2,1)} %win_hbm.1, f32[2,128]{1,0:T(2,128)} %gains.1, bf16[256,256]{1,0:T(8,128)(2,1)} %text.1, s32[1]{0:T(128)S(6)} %copy.8.count, bf16[64,128]{1,0:T(8,128)(2,1)} %bitcast.3), custom_call_target="tpu_custom_call" | custom-call | tf_op jit(solution)/shard_map/sublayer/pallas_call | solution.py:458
  69.8 1.6 %copy.9 = bf16[384,192]{0,1:T(8,128)(2,1)} copy(bf16[384,192]{0,1:T(8,128)(2,1)} %bitcast.2) | data formatting | bytes 294912

commit v5 on v4

--- a/solution.py
+++ b/solution.py
@@ -315,14 +315,14 @@
     def tile(dt, dh):
         return kb[dt, dh], vb[dt, dh], None
 
-    def attend_times(dh, where=None):
+    def attend_times(heights, where, beside_it=()):
         both = jnp.logical_and(earlier[0], earlier[1])
         cases = [(both, (0, 2))] + [(jnp.logical_not(earlier[1 - way]), (2 * way,)) for way in range(2)]
         for case, times in cases:
 
-            @pl.when(case if where is None else jnp.logical_and(case, where))
+            @pl.when(jnp.logical_and(case, where))
             def _(times=times):
-                attend([tile(dt, dh) for dt in times])
+                attend([tile(*at) for at in beside_it] + [tile(dt, dh) for dh in heights for dt in times])
 
     attend([(text_keys, text_values, text_bias), tile(1, 1)], start=True)
     for p in range(2):
@@ -355,14 +355,16 @@
                 remote(ref, ref, kz_s.at[way, p], kz_r.at[way, p], mate).wait_recv()
                 kv_send(*kv_mate(2 * way, p))
 
-    attend_times(1)
     w2_beside(1 - yl).wait_recv()
     w2_mate(c).start()
 
     @pl.when(inner)
     def _():
         land(1, from_across, ky_s, ky_r)
-        attend([tile(1, from_across)])
+
+    outer = jnp.logical_not(inner)
+    attend_times([1], inner, [(1, from_across)])
+    attend_times([1], outer)
 
     for way in range(2):
 
@@ -370,7 +372,7 @@
         def _(way=way):
             land(2 * way, from_mate, kc_s, kc_r)
 
-    attend_times(from_mate)
+    attend_times([from_mate], outer)
 
     for way in range(2):
 
@@ -378,7 +380,7 @@
         def _(way=way):
             land(2 * way, from_across, ky_s, ky_r)
 
-    attend_times(from_across, inner)
+    attend_times([from_mate, from_across], inner)
 
     def halo_drain():
         for p in range(2):

time: 71.6 us -> 71.7 us (level)
  no operation moved by 1% of the time
where the time goes in v5:
time: 71.7 us; the launch traced here: 71.5 us
  Pallas kernels  69.3 us (97%)
  local copies, waits for them, and re-layouts  1.59 us (2%)
    pallas_call x1, Pallas kernels, local(): pl.pallas_call(kernel, out_shape=jax.ShapeDtypeStruct((OUT, TILE), BF16),...  69.3 us
    unnamed x1, local copies, waits for them, and re-layouts  1.59 us

profile of v5, /device:TPU:64, one launch (start us, length us, event | category | flops | bytes accessed | tf_op | source)
XLA Modules:
  0.0 71.5 jit_solution(13018767526994660219)
XLA Ops:
  0.7 69.3 %sublayer.1 = bf16[192,384]{1,0:T(8,128)(2,1)} custom-call(bf16[384,3072]{1,0:T(8,128)(2,1)} %lat_hbm.1, bf16[64,384]{1,0:T(8,128)(2,1)} %win_hbm.1, f32[2,128]{1,0:T(2,128)} %gains.1, bf16[256,256]{1,0:T(8,128)(2,1)} %text.1, s32[1]{0:T(128)S(6)} %copy.8.count, bf16[64,128]{1,0:T(8,128)(2,1)} %bitcast.3), custom_call_target="tpu_custom_call" | custom-call | tf_op jit(solution)/shard_map/sublayer/pallas_call | solution.py:460
  69.9 1.6 %copy.9 = bf16[384,192]{0,1:T(8,128)(2,1)} copy(bf16[384,192]{0,1:T(8,128)(2,1)} %bitcast.2) | data formatting | bytes 294912

commit v6 on v4

--- a/solution.py
+++ b/solution.py
@@ -199,19 +199,19 @@
 
     load_l.wait()
 
-    def multiply(offset):
+    def product(offset):
         h = mod(z - offset, NZ)
         block = w[pl.ds(h, 1)].reshape(4 * RANK, 3 * HD)
-        part_sum = jnp.dot(lat[:, pl.ds(pl.multiple_of(h * 256, 256), 256)], block, preferred_element_type=F32)
-        if offset == 0:
-            acc[...] = part_sum
-        else:
-            acc[...] += part_sum
+        return jnp.dot(lat[:, pl.ds(pl.multiple_of(h * 256, 256), 256)], block, preferred_element_type=F32)
 
     def project(offsets):
         for offset in offsets:
             ring.arrive(offset)
-            multiply(offset)
+        total = sum(product(offset) for offset in offsets)
+        if offsets == [0]:
+            acc[...] = total
+        else:
+            acc[...] += total
 
     first, second, third_ = ORDER[1:5], ORDER[5:9], ORDER[9:]
     for offset in first:

time: 71.6 us -> 71.3 us (level)
  the two profiles are of different devices: /device:TPU:64 before, /device:TPU:72 now
where the time goes in v6:
time: 71.3 us; the launch traced here: 71.1 us
  Pallas kernels  68.9 us (97%)
  local copies, waits for them, and re-layouts  1.59 us (2%)
    pallas_call x1, Pallas kernels, local(): pl.pallas_call(kernel, out_shape=jax.ShapeDtypeStruct((OUT, TILE), BF16),...  68.9 us
    unnamed x1, local copies, waits for them, and re-layouts  1.59 us

profile of v6, /device:TPU:72, one launch (start us, length us, event | category | flops | bytes accessed | tf_op | source)
XLA Modules:
  0.0 71.1 jit_solution(8831902046699965369)
XLA Ops:
  0.7 68.9 %sublayer.1 = bf16[192,384]{1,0:T(8,128)(2,1)} custom-call(bf16[384,3072]{1,0:T(8,128)(2,1)} %lat_hbm.1, bf16[64,384]{1,0:T(8,128)(2,1)} %win_hbm.1, f32[2,128]{1,0:T(2,128)} %gains.1, bf16[256,256]{1,0:T(8,128)(2,1)} %text.1, s32[1]{0:T(128)S(6)} %copy.8.count, bf16[64,128]{1,0:T(8,128)(2,1)} %bitcast.3), custom_call_target="tpu_custom_call" | custom-call | tf_op jit(solution)/shard_map/sublayer/pallas_call | solution.py:458
  69.5 1.6 %copy.9 = bf16[384,192]{0,1:T(8,128)(2,1)} copy(bf16[384,192]{0,1:T(8,128)(2,1)} %bitcast.2) | data formatting | bytes 294912
